TPU v7x, 256 devices: a whole 4x4x8 slice. The times are simulated.
256 devices in a mesh: dp: 16 (over y_hi, x, core), cent: 8 (over z), rep: 2 (over y_lo).
Axes of the slice: x: 4, y: 4 (y_hi: 2, y_lo: 2; y = y_hi * 2 + y_lo), z: 8, core: 2. Of those that a mesh axis runs over, the one named last changes fastest.
Arguments:
- points: bfloat16 [16384, 1024], P('dp'), may hold values from -6 to 6
- centroids: bfloat16 [8, 4096, 1024], P('rep', 'cent'), may hold values from -1.5 to 1.5
- counts: int32 [8, 16384], P('rep', 'dp'), may hold values from 0 to 5, as said below
Outputs:
- updated: bfloat16 [8, 4096, 1024], P('rep', 'cent', 'dp')
- bagged_score: float32 [16384], P('dp')
Inputs may be any that keep to these rules, and one draw needn't show every extreme that they name: `counts`: in every replicate some point has count 5.
All inputs are finite; a program needn't handle non-finite values.
Results may differ from a plain program's by a relative error of at most 0.0045.
Values sent between devices are 32-bit elements; how exact they have to be, the bound alone decides.
A program may use at most 64 MiB of HBM per device.

v0:
```python
import math

import jax
import jax.numpy as jnp
from jax import lax
from jax.sharding import PartitionSpec as P

prior_weight = 1.0


def shards(points, centroids, counts):
    rep_local, cent_local, features = centroids.shape
    squares = jnp.sum(jnp.square(centroids.astype(jnp.float32)), axis=2)
    logits = (
        jnp.einsum("nd,rkd->rnk", points, centroids, preferred_element_type=jnp.float32)
        - 0.5 * squares[:, None, :]
    )
    row_top = lax.pmax(jnp.max(logits, axis=2), "cent")
    row_total = lax.psum(jnp.sum(jnp.exp(logits - row_top[:, :, None]), axis=2), "cent")
    weights = counts.astype(jnp.float32)
    weighted = (
        jnp.exp(logits - row_top[:, :, None]) / row_total[:, :, None] * weights[:, :, None]
    ).astype(jnp.bfloat16)
    cluster_mass = lax.psum(jnp.sum(weighted.astype(jnp.float32), axis=1), "dp")
    slab_width = features // lax.axis_size("dp")
    position = lax.axis_index("dp")
    moment_sums = jnp.einsum("rnk,nd->rkd", weighted, points, preferred_element_type=jnp.float32)
    moments = lax.psum_scatter(moment_sums, "dp", scatter_dimension=2, tiled=True)
    own_slice = lax.dynamic_slice_in_dim(centroids, position * slab_width, slab_width, 2).astype(
        jnp.float32
    )
    updated = (
        (moments + prior_weight * own_slice) / (cluster_mass[:, :, None] + prior_weight)
    ).astype(jnp.bfloat16)
    log_total = row_top + jnp.log(row_total)
    summed = lax.psum(jnp.sum(log_total, axis=0), "rep")
    replicas = rep_local * lax.axis_size("rep")
    clusters = cent_local * lax.axis_size("cent")
    bagged_score = summed / replicas - math.log(clusters)
    return (updated, bagged_score)


def solution(mesh):
    return jax.shard_map(
        shards,
        mesh=mesh,
        in_specs=(P("dp", None), P("rep", "cent", None), P("rep", "dp")),
        out_specs=(P("rep", "cent", "dp"), P("dp")),
        check_vma=False,
    )
```

profile of v0, /device:TPU:2, one launch (start us, length us, event | category | flops | bytes accessed | tf_op | source)
XLA Modules:
  0.0 212.5 jit_solution(8605060416636865341)
XLA Ops:
  7.2 0.0 copy-start
  7.2 0.0 reduce-scatter.2.cloned.1.call-start
  7.2 3.2 %multiply_reduce_fusion = f32[4,512]{1,0:T(4,128)S(1)} fusion(bf16[4,512,1024]{2,1,0:T(8,128)(2,1)} %param.4), kind=kLoop, calls=%fused_computation.5 | loop fusion | flops 6289408 | bytes 4202496 | tf_op jit(solution)/shard_map/reduce_sum | solution.py:13
  10.5 0.0 copy-done
  10.5 9.1 %bitcast_reduce_fusion = (f32[4,1024]{1,0:T(4,128)S(1)}, f32[4,512,1024]{2,1,0:T(8,128)}) fusion(f32[4,512]{1,0:T(4,128)S(1)} %broadcast_multiply_fusion, bf16[4,512,1024]{2,1,0:T(8,128)(2,1)} %param.4, bf16[1024,1024]{1,0:T(8,128)(2,1)S(1)} %copy-done), kind=kOutput, calls=%fused_computation.1 | convolution fusion | flops 4299157504 | bytes 14704640 | tf_op jit(solution)/shard_map/nd,rkd->rnk/dot_general | solution.py:15
  19.5 0.0 copy-start.1
  19.5 32.9 %pmax.7 = f32[4,1024]{1,0:T(4,128)S(1)} all-reduce(f32[4,1024]{1,0:T(4,128)S(1)} %get-tuple-element.4), channel_id=1, replica_groups=mesh['dp'=16,'cent'=8,'rep'=2] {'cent'}, use_global_device_ids=true, to_apply=%region_2.0 | all-reduce | flops 4096 | bytes 32768 | tf_op jit(solution)/shard_map/pmax | solution.py:18
  52.4 4.2 %fusion.1 = f32[4,1024]{1,0:T(4,128)S(1)} fusion(f32[4,512,1024]{2,1,0:T(8,128)} %get-tuple-element.5, f32[4,1024]{1,0:T(4,128)S(1)} %pmax.7, f32[4,512]{1,0:T(4,128)S(1)} %broadcast_multiply_fusion), kind=kLoop, calls=%fused_computation.6 | loop fusion | flops 6287360 | bytes 8429568 | tf_op jit(solution)/shard_map/reduce_sum | solution.py:19
  56.7 27.0 %psum.21 = f32[4,1024]{1,0:T(4,128)S(1)} all-reduce(f32[4,1024]{1,0:T(4,128)S(1)} %fusion.1), channel_id=1, replica_groups=mesh['dp'=16,'cent'=8,'rep'=2] {'cent'}, use_global_device_ids=true, to_apply=%region_4.0 | all-reduce | flops 4096 | bytes 32768 | tf_op jit(solution)/shard_map/psum | solution.py:19
  83.7 0.0 copy-done.1
  83.7 4.8 %convert_reduce_fusion = (f32[4,512]{1,0:T(4,128)S(1)}, bf16[4,1024,512]{1,2,0:T(8,128)(2,1)S(1)}) fusion(f32[4,1024]{1,0:T(4,128)S(1)} %convert_element_type.19, f32[4,1024]{1,0:T(4,128)S(1)} %psum.21, f32[4,1024]{1,0:T(4,128)S(1)} %pmax.7, f32[4,512,1024]{2,1,0:T(8,128)} %get-tuple-element.5, f32[4,512]{1,0:T(4,128)S(1)} %broadcast_multiply_fusion), kind=kLoop, calls=%fused_computation.3 | loop fusion | flops 14678016 | bytes 12648448 | tf_op jit(solution)/shard_map/reduce_sum | solution.py:24
  88.5 7.0 %fusion.2 = f32[4,512,1024]{1,2,0:T(8,128)} fusion(bf16[4,1024,512]{1,2,0:T(8,128)(2,1)S(1)} %get-tuple-element.3, bf16[1024,1024]{1,0:T(8,128)(2,1)S(1)} %copy-done), kind=kOutput, calls=%fused_computation.7 | convolution fusion | flops 4294967296 | bytes 14680064 | tf_op jit(solution)/shard_map/rnk,nd->rkd/dot_general | solution.py:27
  95.5 0.0 reduce-scatter.2.cloned.1.call-update
  95.5 1.3 constant_dynamic-slice_fusion
  96.8 0.2 copy.11
  97.0 4.9 %psum.23 = f32[1024]{0:T(1024)S(1)} all-reduce(f32[1024]{0:T(1024)S(1)} %add_reduce_fusion), channel_id=1, replica_groups=mesh['dp'=16,'cent'=8,'rep'=2] {'rep'}, use_global_device_ids=true, to_apply=%region_9.0 | all-reduce | flops 1024 | bytes 8192 | tf_op jit(solution)/shard_map/psum | solution.py:36
  101.9 28.3 %psum.22 = f32[4,512]{1,0:T(4,128)S(1)} all-reduce(f32[4,512]{1,0:T(4,128)S(1)} %get-tuple-element.2), channel_id=1, replica_groups=mesh['dp'=16,'cent'=8,'rep'=2] {'dp'}, use_global_device_ids=true, to_apply=%region_7.0 | all-reduce | flops 2048 | bytes 16384 | tf_op jit(solution)/shard_map/psum | solution.py:24
  130.2 0.6 multiply_add_fusion
  130.8 73.0 %reduce-scatter.2.cloned.1.call-done = f32[4,512,64]{1,2,0:T(8,128)} async-done(((f32[4,512,1024]{1,2,0:T(8,128)}), f32[4,512,64]{1,2,0:T(8,128)}) %reduce-scatter.2.cloned.1.call-update) | async-done | bytes 524304 | tf_op jit(solution)/shard_map/reduce_scatter | solution.py:28
  203.8 1.8 divide_convert_fusion
  (4 shorter events, 0.0 us)
Async XLA Ops:
  7.2 3.3 %copy-start = (bf16[1024,1024]{1,0:T(8,128)(2,1)S(1)}, bf16[1024,1024]{1,0:T(8,128)(2,1)}, u32[]{:S(2)}) copy-start(bf16[1024,1024]{1,0:T(8,128)(2,1)} %param.3) | copy-start | bytes 6291460
  7.2 196.6 %reduce-scatter.2.cloned.1.call-start = ((), (), s32[]{:S(2)}) async-start(), calls=%async_computation.1 | async-start | bytes 8912896 | tf_op jit(solution)/shard_map/reduce_scatter | solution.py:28
  19.5 64.2 %copy-start.1 = (s32[4,1024]{1,0:T(4,128)S(1)}, s32[4,1024]{1,0:T(4,128)}, u32[]{:S(2)}) copy-start(s32[4,1024]{1,0:T(4,128)} %param.5) | copy-start | bytes 49156
Sparse Core Ops, SparseCore 0:
  95.6 108.1 reduce-scatter.1
where the time goes:
time: 213 us; the launch traced here: 212 us
  blocking collectives  93.1 us (44%)
  waiting for transfers between devices  73 us (34%)
  matrix products  16.1 us (8%)
  other arithmetic  14.7 us (7%)
  between operations  14.1 us (7%)
    reduce_scatter x1, waiting for transfers between devices, shards(): lax.psum_scatter(moment_sums, 'dp', scatter_dimension=2, tiled=True)  73 us
    pmax x1, blocking collectives, shards(): row_top = lax.pmax(jnp.max(logits, axis=2), 'cent')  32.9 us
    psum x1, blocking collectives, shards(): cluster_mass = lax.psum(jnp.sum(weighted.astype(jnp.float32), axis=1), 'dp')  28.3 us
    psum x1, blocking collectives, shards(): lax.psum(jnp.sum(jnp.exp(logits - row_top[:, :, None]), axis=2), 'cent')  27 us
    dot_general x1, matrix products, shards(): jnp.einsum('nd,rkd->rnk', points, centroids, preferred_element_type=jnp.f...  9.08 us
    dot_general x1, matrix products, shards(): jnp.einsum('rnk,nd->rkd', weighted, points, preferred_element_type=jnp.fl...  6.97 us
    psum x1, blocking collectives, shards(): summed = lax.psum(jnp.sum(log_total, axis=0), 'rep')  4.95 us
    reduce_sum x1, other arithmetic, shards(): cluster_mass = lax.psum(jnp.sum(weighted.astype(jnp.float32), axis=1), 'dp')  4.79 us
  transfers between devices with their start and end apart: 1, of which 1 were waited for; matrix products, arithmetic and copies ran while one was open for 1% of the time, Pallas kernels for 0%

commit v1 on v0

v1 whole, which is shorter than its diff:
```python
import math

import jax
import jax.numpy as jnp
from jax import lax
from jax.experimental import pallas as pl
from jax.experimental.pallas import tpu as pltpu
from jax.sharding import PartitionSpec as P

MESH = pl.DeviceIdType.MESH
F32 = jnp.float32
REPS = 4
NK = 512
HALF = 256
D = 1024
N = 1024
RA = 144
RB = HALF - RA
HB = RB // 2
NT = 256
OFFS = (2, 1, 3, 0)
prior_weight = 1.0

REL_P, REL_M, PLA_P, PLA_M, AUG_P, AUG_M, Y_A, Y_B, BREL_P, BREL_M, BPLA_P, BPLA_M, BAUG_P, BAUG_M = range(14)


def pack(top, low):
    first = lax.broadcasted_iota(jnp.int32, top.shape, 1) < 64
    swapped = pltpu.roll(jnp.where(first, low, top), 64, 1)
    return jnp.where(first, top, swapped), jnp.where(first, swapped, low)


def kernel(
    p_hbm, c_hbm, n_hbm, u_ref, b_ref,
    p_v, c_v, n_v, e_v, w_v, hs_v, st, mp, cr, sa, sb,
    ra_m, ra_p, da_m, da_p, ya, yb, rb_m, rb_p, db_m, db_p, mass, lt,
    ld, zs, zr, cs, crs, xs, xr, ms, mr, ls, lr,
):
    p = lax.axis_index("dp")
    z = lax.axis_index("cent")
    l = lax.axis_index("rep")
    c = p % 2
    x = (p // 2) % 4
    yh = p // 8
    sib = (p + 1 - 2 * c, z, l)
    xp = (yh * 8 + ((x + 1) % 4) * 2 + c, z, l)
    xm = (yh * 8 + ((x + 3) % 4) * 2 + c, z, l)
    y2 = ((1 - yh) * 8 + x * 2 + c, z, l)
    other = (p, z, 1 - l)

    loads = [pltpu.make_async_copy(p_hbm, p_v, ld.at[0])]
    loads.append(pltpu.make_async_copy(n_hbm, n_v, ld.at[1]))
    for r in range(REPS):
        loads.append(pltpu.make_async_copy(c_hbm.at[r], c_v.at[r], ld.at[2 + r]))
    for i in (2, 0, 3, 4, 5, 1):
        loads[i].start()

    barrier = pltpu.get_barrier_semaphore()
    for j in range(1, 16):
        pl.semaphore_signal(barrier, inc=1, device_id=((p + j) % 16, z, l), device_id_type=MESH)
    for j in range(1, 8):
        pl.semaphore_signal(barrier, inc=1, device_id=(p, (z + j) % 8, l), device_id_type=MESH)
    pl.semaphore_signal(barrier, inc=1, device_id=other, device_id_type=MESH)

    sent = []

    def send(src, dst, ssem, rsem, dev):
        copy = pltpu.make_async_remote_copy(
            src_ref=src, dst_ref=dst, send_sem=ssem, recv_sem=rsem, device_id=dev, device_id_type=MESH
        )
        copy.start()
        sent.append(copy)
        return copy

    def logits(r):
        loads[2 + r].wait()
        if r == 0:
            loads[0].wait()
        for i in range(0, NK, 64):
            block = c_v[r, i : i + 64, :].astype(F32)
            hs_v[i : i + 64, :] = jnp.broadcast_to(
                0.5 * jnp.sum(block * block, axis=1, keepdims=True), (64, 128)
            )

        def tile(t, carry):
            cols = pl.ds(pl.multiple_of(t * NT, NT), NT)
            e_v[r, :, cols] = lax.dot_general(
                c_v[r], p_v[cols, :], (((1,), (1,)), ((), ())), preferred_element_type=F32
            )
            top = None
            for i in range(0, NK, 64):
                half = hs_v[i : i + 64, :]
                block = e_v[r, i : i + 64, cols] - jnp.concatenate([half, half], axis=1)
                e_v[r, i : i + 64, cols] = block
                part = jnp.max(block.reshape(8, 8, NT), axis=0)
                top = part if top is None else jnp.maximum(top, part)
            top = jnp.max(top, axis=0, keepdims=True)
            total = None
            for i in range(0, NK, 64):
                block = jnp.exp(e_v[r, i : i + 64, cols] - top)
                e_v[r, i : i + 64, cols] = block
                part = jnp.sum(block.reshape(8, 8, NT), axis=0)
                total = part if total is None else total + part
            st[r, z, 0:1, cols] = top
            st[r, z, 1:2, cols] = jnp.sum(total, axis=0, keepdims=True)
            return carry

        lax.fori_loop(0, N // NT, tile, 0)

    zc = {}

    def send_stats(r):
        for j in range(1, 8):
            zc[r, j] = send(st.at[r, z], st.at[r, z], zs.at[r, j], zr.at[r, j], (p, (z + j) % 8, l))

    cc = {}

    def moments(r):
        for j in range(1, 8):
            zc[r, j].wait_recv()
        top = st[r, 0, 0:1, :]
        for j in range(1, 8):
            top = jnp.maximum(top, st[r, j, 0:1, :])
        total = jnp.zeros_like(top)
        for j in range(8):
            total += st[r, j, 1:2, :] * jnp.exp(st[r, j, 0:1, :] - top)
        scale = jnp.exp(st[r, z, 0:1, :] - top) / total * n_v[r : r + 1, :].astype(F32)
        log_total = top + jnp.log(total)
        if r == 0:
            lt[l, :, :] = log_total
        else:
            lt[l, :, :] += log_total
        for i in range(0, NK, 32):
            w_v[i : i + 32, :] = (e_v[r, i : i + 32, :] * scale).astype(jnp.bfloat16)
        for g in range(4):
            xx = (x + OFFS[g]) % 4
            lo = pl.ds(pl.multiple_of(xx * 128, 128), 128)
            hi = pl.ds(pl.multiple_of(512 + xx * 128, 128), 128)
            block = jnp.concatenate([p_v[:, lo], p_v[:, hi]], axis=1)
            out = jnp.dot(w_v[...], block, preferred_element_type=F32)
            for h in range(2):
                part = out[:, h * 128 : (h + 1) * 128]
                zero, one = pack(part[:HALF], part[HALF:])
                mp[r, 0, xx, h, :, :] = zero
                mp[r, 1, xx, h, :, :] = one
            cc[r, g] = send(mp.at[r, 1 - c, xx], cr.at[r, xx], cs.at[r, g], crs.at[r, g], sib)
        sums = jnp.dot(w_v[...], jnp.ones((N, 128), jnp.bfloat16), preferred_element_type=F32)
        eye = lax.broadcasted_iota(jnp.int32, (128, 128), 0) == lax.broadcasted_iota(
            jnp.int32, (128, 128), 1
        )
        for g in range(4):
            mass[p, r * 4 + g : r * 4 + g + 1, :] = jnp.sum(
                jnp.where(eye, sums[g * 128 : (g + 1) * 128], 0.0), axis=0, keepdims=True
            )

    xc = {}

    def xsend(r, i, src, dst, dev):
        xc[r, i] = send(src, dst, xs.at[r, i], xr.at[r, i], dev)

    x_opp, x_next, x_prev = (x + 2) % 4, (x + 1) % 4, (x + 3) % 4

    def stage1(r):
        for g in range(4):
            xx = (x + OFFS[g]) % 4
            cc[r, g].wait_recv()
            for h in range(2):
                sa[r, xx, h, :, :] = mp[r, c, xx, h, :RA, :] + cr[r, xx, h, :RA, :]
                sb[r, h, xx, :, :] = mp[r, c, xx, h, RA:, :] + cr[r, xx, h, RA:, :]
            if g == 0:
                xsend(r, REL_P, sa.at[r, x_opp, 0], ra_m.at[r], xp)
                xsend(r, REL_M, sa.at[r, x_opp, 1], ra_p.at[r], xm)
            if g == 1:
                xsend(r, PLA_P, sa.at[r, x_next, 1], da_m.at[r, 1], xp)
            if g == 2:
                xsend(r, PLA_M, sa.at[r, x_prev, 0], da_p.at[r, 0], xm)
        xsend(r, Y_B, sb.at[r, 1 - yh], yb.at[r], y2)

    def stage2(r):
        xc[r, REL_P].wait_recv()
        sa[r, x_next, 0, :, :] += ra_m[r]
        xsend(r, AUG_P, sa.at[r, x_next, 0], da_m.at[r, 0], xp)
        xc[r, REL_M].wait_recv()
        sa[r, x_prev, 1, :, :] += ra_p[r]
        xsend(r, AUG_M, sa.at[r, x_prev, 1], da_p.at[r, 1], xm)
        xc[r, Y_B].wait_recv()
        sb[r, yh, x_opp, :, :] += yb[r, x_opp]
        xsend(r, BREL_P, sb.at[r, yh, x_opp, pl.ds(0, HB)], rb_m.at[r], xp)
        xsend(r, BREL_M, sb.at[r, yh, x_opp, pl.ds(HB, HB)], rb_p.at[r], xm)
        sb[r, yh, x_next, :, :] += yb[r, x_next]
        xsend(r, BPLA_P, sb.at[r, yh, x_next, pl.ds(HB, HB)], db_m.at[r, pl.ds(HB, HB)], xp)
        sb[r, yh, x_prev, :, :] += yb[r, x_prev]
        xsend(r, BPLA_M, sb.at[r, yh, x_prev, pl.ds(0, HB)], db_p.at[r, pl.ds(0, HB)], xm)

    def stage3(r):
        for i in (PLA_P, PLA_M, AUG_P, AUG_M):
            xc[r, i].wait_recv()
        for h in range(2):
            sa[r, x, h, :, :] += da_m[r, h] + da_p[r, h]
        xsend(r, Y_A, sa.at[r, x, 1 - yh], ya.at[r], y2)
        xc[r, BREL_P].wait_recv()
        sb[r, yh, x_next, :HB, :] += rb_m[r]
        xsend(r, BAUG_P, sb.at[r, yh, x_next, pl.ds(0, HB)], db_m.at[r, pl.ds(0, HB)], xp)
        xc[r, BREL_M].wait_recv()
        sb[r, yh, x_prev, HB:, :] += rb_p[r]
        xsend(r, BAUG_M, sb.at[r, yh, x_prev, pl.ds(HB, HB)], db_p.at[r, pl.ds(HB, HB)], xm)

    mc = {}

    def send_mass():
        for j in range(1, 16):
            mc[j] = send(mass.at[p], mass.at[p], ms.at[j], mr.at[j], ((p + j) % 16, z, l))
        mc[0] = send(lt.at[l], lt.at[l], ls, lr, other)

    masses = []

    def receive_mass():
        for j in range(1, 16):
            mc[j].wait_recv()
        total = mass[0]
        for j in range(1, 16):
            total += mass[j]
        masses.append(total)
        mc[0].wait_recv()
        b_ref[...] = (lt[0] + lt[1]) / 8.0 - math.log(4096)

    def stage4(r):
        q = pl.ds(pl.multiple_of((yh * 4 + x) * 128, 128), 128)
        total = masses[0]
        row = lax.broadcasted_iota(jnp.int32, (128, 128), 0)
        cols = []
        for i in range(2):
            a = total[r * 4 + i : r * 4 + i + 1, :]
            b = total[r * 4 + 2 + i : r * 4 + 3 + i, :]
            cols.append(jnp.where(row < 64, a, b).T)
        weight = jnp.concatenate(cols, axis=0) + prior_weight
        zero, one = pack(c_v[r, :HALF, q].astype(F32), c_v[r, HALF:, q].astype(F32))
        own = prior_weight * jnp.where(jnp.full((HALF, 128), c, jnp.int32) == 0, zero, one)
        for i in (BPLA_P, BPLA_M, BAUG_P, BAUG_M):
            xc[r, i].wait_recv()
        low = sb[r, yh, x] + yb[r, x] + db_m[r] + db_p[r]
        u_ref[r, RA:, :] = ((low + own[RA:]) / weight[RA:]).astype(jnp.bfloat16)
        xc[r, Y_A].wait_recv()
        high = sa[r, x, yh] + ya[r]
        u_ref[r, :RA, :] = ((high + own[:RA]) / weight[:RA]).astype(jnp.bfloat16)

    logits(0)
    pl.semaphore_wait(barrier, 23)
    send_stats(0)
    for r in range(1, REPS):
        logits(r)
        send_stats(r)
    loads[1].wait()
    moments(0)
    stage1(0)
    moments(1)
    stage1(1)
    stage2(0)
    moments(2)
    stage1(2)
    stage2(1)
    stage3(0)
    moments(3)
    send_mass()
    stage1(3)
    stage2(2)
    stage3(1)
    receive_mass()
    stage4(0)
    stage2(3)
    stage3(2)
    stage4(1)
    stage3(3)
    stage4(2)
    stage4(3)
    for copy in sent:
        copy.wait_send()


def shards(points, centroids, counts):
    dma = pltpu.SemaphoreType.DMA
    packed, bagged = pl.pallas_call(
        kernel,
        out_shape=(
            jax.ShapeDtypeStruct((REPS, HALF, 128), jnp.bfloat16),
            jax.ShapeDtypeStruct((1, N), F32),
        ),
        in_specs=[pl.BlockSpec(memory_space=pl.ANY)] * 3,
        out_specs=[pl.BlockSpec(memory_space=pltpu.VMEM)] * 2,
        scratch_shapes=[
            pltpu.VMEM((N, D), jnp.bfloat16),
            pltpu.VMEM((REPS, NK, D), jnp.bfloat16),
            pltpu.VMEM((REPS, N), jnp.int32),
            pltpu.VMEM((REPS, NK, N), F32),
            pltpu.VMEM((NK, N), jnp.bfloat16),
            pltpu.VMEM((NK, 128), F32),
            pltpu.VMEM((REPS, 8, 2, N), F32),
            pltpu.VMEM((REPS, 2, 4, 2, HALF, 128), F32),
            pltpu.VMEM((REPS, 4, 2, HALF, 128), F32),
            pltpu.VMEM((REPS, 4, 2, RA, 128), F32),
            pltpu.VMEM((REPS, 2, 4, RB, 128), F32),
            pltpu.VMEM((REPS, RA, 128), F32),
            pltpu.VMEM((REPS, RA, 128), F32),
            pltpu.VMEM((REPS, 2, RA, 128), F32),
            pltpu.VMEM((REPS, 2, RA, 128), F32),
            pltpu.VMEM((REPS, RA, 128), F32),
            pltpu.VMEM((REPS, 4, RB, 128), F32),
            pltpu.VMEM((REPS, HB, 128), F32),
            pltpu.VMEM((REPS, HB, 128), F32),
            pltpu.VMEM((REPS, RB, 128), F32),
            pltpu.VMEM((REPS, RB, 128), F32),
            pltpu.VMEM((16, 4 * REPS, 128), F32),
            pltpu.VMEM((2, 1, N), F32),
            dma((2 + REPS,)),
            dma((REPS, 8)),
            dma((REPS, 8)),
            dma((REPS, 4)),
            dma((REPS, 4)),
            dma((REPS, 14)),
            dma((REPS, 14)),
            dma((16,)),
            dma((16,)),
            dma,
            dma,
        ],
        compiler_params=pltpu.CompilerParams(
            collective_id=0, has_side_effects=True, vmem_limit_bytes=56 * 1024 * 1024
        ),
    )(points, centroids, counts)
    updated = packed.reshape(REPS, HALF, 2, 64).transpose(0, 2, 1, 3).reshape(REPS, NK, 64)
    return updated, bagged.reshape(N)


def solution(mesh):
    return jax.shard_map(
        shards,
        mesh=mesh,
        in_specs=(P("dp", None), P("rep", "cent", None), P("rep", "dp")),
        out_specs=(P("rep", "cent", "dp"), P("dp")),
        check_vma=False,
    )
```

time: 213 us -> 62.6 us (0.29)
  blocking collectives: 93.1 us -> 0 us
  waiting for transfers between devices: 73 us -> 0 us
  Pallas kernels: 0 us -> 58.6 us
  matrix products: 16.1 us -> 0 us
  other arithmetic: 14.7 us -> 0 us
  between operations: 14.1 us -> 0.65 us
    reduce_scatter x1 -> x0, waiting for transfers between devices: 73 us -> none  [shards(): lax.psum_scatter(moment_sums, 'dp', scatter_dimension=2, tiled=True)]
    psum x3 -> x0, blocking collectives: 60.2 us -> none  [the longest x1 28.3 us: shards(): cluster_mass = lax.psum(jnp.sum(weighted.astype(jnp.float32), axis=1), 'dp')]
    pallas_call x0 -> x1, Pallas kernels: none -> 58.6 us  [shards(): pl.pallas_call(kernel, out_shape=(jax.ShapeDtypeStruct((REPS, HALF, 128),...]
    pmax x1 -> x0, blocking collectives: 32.9 us -> none  [shards(): row_top = lax.pmax(jnp.max(logits, axis=2), 'cent')]
    dot_general x2 -> x0, matrix products: 16.1 us -> none  [the longest x1 9.08 us: shards(): jnp.einsum('nd,rkd->rnk', points, centroids, preferred_element_type=jnp.f...]
    reduce_sum x4 -> x0, other arithmetic: 12.3 us -> none  [the longest x1 4.79 us: shards(): cluster_mass = lax.psum(jnp.sum(weighted.astype(jnp.float32), axis=1), 'dp')]
  transfers between devices with their start and end apart: 1 -> 0, of which waited for: 1 -> 0; matrix products, arithmetic and copies ran while one was open for 1% -> 0% of each run, Pallas kernels for 0% -> 0%
where the time goes in v1:
time: 62.6 us; the launch traced here: 62.3 us
  Pallas kernels  58.6 us (94%)
  local copies, waits for them, and re-layouts  3.09 us (5%)
  between operations  0.65 us (1%)
    pallas_call x1, Pallas kernels, shards(): pl.pallas_call(kernel, out_shape=(jax.ShapeDtypeStruct((REPS, HALF, 128),...  58.6 us
    unnamed x1, local copies, waits for them, and re-layouts  1.28 us

profile of v1, /device:TPU:2, one launch (start us, length us, event | category | flops | bytes accessed | tf_op | source)
XLA Modules:
  0.0 62.3 jit_solution(1708281761832797539)
XLA Ops:
  0.6 58.6 %shard_map.50 = (bf16[4,256,128]{2,1,0:T(8,128)(2,1)}, f32[1,1024]{1,0:T(1,128)}) custom-call(bf16[1024,1024]{1,0:T(8,128)(2,1)} %p_hbm.1, bf16[4,512,1024]{2,1,0:T(8,128)(2,1)} %c_hbm.1, s32[4,1024]{1,0:T(4,128)} %n_hbm.1), custom_call_target="tpu_custom_call" | custom-call | tf_op jit(solution)/shard_map/pallas_call | solution.py:282
  59.2 1.1 %copy.7 = bf16[4,256,128]{1,2,0:T(8,128)(2,1)S(1)} copy(bf16[4,256,128]{2,1,0:T(8,128)(2,1)} %get-tuple-element.4) | data formatting | bytes 524288 | tf_op jit(solution)/shard_map/pallas_call | solution.py:282
  60.3 0.7 %copy.9 = bf16[4,2,8,8,256]{4,3,1,2,0:T(8,128)(2,1)} copy(bf16[4,2,8,8,256]{4,3,2,1,0:T(8,128)(2,1)S(1)} %bitcast.6) | data formatting | bytes 524288 | tf_op jit(solution)/shard_map/reshape | solution.py:330
  61.0 1.3 %copy.11 = f32[1024]{0:T(1024)} copy(f32[1024]{0:T(1024)} %bitcast.8) | data formatting | bytes 8192

commit v2 on v1

v2 whole, which is shorter than its diff:
```python
import math

import jax
import jax.numpy as jnp
from jax import lax
from jax.experimental import pallas as pl
from jax.experimental.pallas import tpu as pltpu
from jax.sharding import PartitionSpec as P

MESH = pl.DeviceIdType.MESH
F32 = jnp.float32
REPS = 4
NK = 512
HALF = 256
D = 1024
N = 1024
RA = 144
RB = HALF - RA
HB = RB // 2
NT = 256
LAG = 3
OFFS = (2, 1, 3, 0)
prior_weight = 1.0

REL_P, REL_M, PLA_P, PLA_M, AUG_P, AUG_M, Y_A, BREL_P, BREL_M, BPLA_P, BPLA_M, BAUG_P, BAUG_M, Y_B = range(14)
EXCHANGES = Y_B + 4

EARLY = {11: [("aug_a", 0)], 15: [("aug_a", 1)]}
LATE = [
    ("rel_b", 0), ("aug_a", 2), ("y_a", 0), ("rel_b", 1), ("aug_a", 3), ("aug_b", 0), ("y_a", 1), ("rel_b", 2),
    ("aug_b", 1), ("y_a", 2), ("rel_b", 3), ("aug_b", 2), ("y_a", 3), ("finish", 0), ("finish", 1), ("aug_b", 3),
    ("finish", 2), ("finish", 3),
]


def pack(top, low):
    first = lax.broadcasted_iota(jnp.int32, top.shape, 1) < 64
    swapped = pltpu.roll(jnp.where(first, low, top), 64, 1)
    return jnp.where(first, top, swapped), jnp.where(first, swapped, low)


def kernel(
    p_hbm, c_hbm, n_hbm, u_ref, b_ref,
    p_v, c_v, n_v, e_v, w_v, hs_v, sc_v, st, mp, cr, sa, sb,
    ra_m, ra_p, da_m, da_p, ya, yb, rb_m, rb_p, db_m, db_p, mass, lt,
    ld, zs, zr, cs, crs, xs, xr, ms, mr, ls, lr,
):
    p = lax.axis_index("dp")
    z = lax.axis_index("cent")
    l = lax.axis_index("rep")
    c = p % 2
    x = (p // 2) % 4
    yh = p // 8
    sib = (p + 1 - 2 * c, z, l)
    xp = (yh * 8 + ((x + 1) % 4) * 2 + c, z, l)
    xm = (yh * 8 + ((x + 3) % 4) * 2 + c, z, l)
    y2 = ((1 - yh) * 8 + x * 2 + c, z, l)
    other = (p, z, 1 - l)

    loads = [pltpu.make_async_copy(p_hbm, p_v, ld.at[0])]
    loads.append(pltpu.make_async_copy(n_hbm, n_v, ld.at[1]))
    for r in range(REPS):
        loads.append(pltpu.make_async_copy(c_hbm.at[r], c_v.at[r], ld.at[2 + r]))
    for i in (2, 0, 3, 4, 5, 1):
        loads[i].start()

    barrier = pltpu.get_barrier_semaphore()
    for j in range(1, 16):
        pl.semaphore_signal(barrier, inc=1, device_id=((p + j) % 16, z, l), device_id_type=MESH)
    for j in range(1, 8):
        pl.semaphore_signal(barrier, inc=1, device_id=(p, (z + j) % 8, l), device_id_type=MESH)
    pl.semaphore_signal(barrier, inc=1, device_id=other, device_id_type=MESH)

    sent = []

    def send(src, dst, ssem, rsem, dev):
        copy = pltpu.make_async_remote_copy(
            src_ref=src, dst_ref=dst, send_sem=ssem, recv_sem=rsem, device_id=dev, device_id_type=MESH
        )
        copy.start()
        sent.append(copy)
        return copy

    def logits(r):
        loads[2 + r].wait()
        if r == 0:
            loads[0].wait()
        for i in range(0, NK, 64):
            block = c_v[r, i : i + 64, :].astype(F32)
            hs_v[i : i + 64, :] = jnp.broadcast_to(
                0.5 * jnp.sum(block * block, axis=1, keepdims=True), (64, 128)
            )

        for t in range(0, N, NT):
            cols = slice(t, t + NT)
            half = hs_v[...]
            tile = lax.dot_general(
                c_v[r], p_v[cols, :], (((1,), (1,)), ((), ())), preferred_element_type=F32
            ) - jnp.concatenate([half, half], axis=1)
            top = jnp.max(tile, axis=0, keepdims=True)
            tile = jnp.exp(tile - top)
            e_v[r, :, cols] = tile
            st[r, z, 0:1, cols] = top
            st[r, z, 1:2, cols] = jnp.sum(tile, axis=0, keepdims=True)

    zc = {}

    def send_stats(r):
        for j in range(1, 8):
            zc[r, j] = send(st.at[r, z], st.at[r, z], zs.at[r, j], zr.at[r, j], (p, (z + j) % 8, l))

    cc = {}

    def scale(r):
        for j in range(1, 8):
            zc[r, j].wait_recv()
        top = st[r, 0, 0:1, :]
        for j in range(1, 8):
            top = jnp.maximum(top, st[r, j, 0:1, :])
        total = jnp.zeros_like(top)
        for j in range(8):
            total += st[r, j, 1:2, :] * jnp.exp(st[r, j, 0:1, :] - top)
        sc_v[r, :, :] = jnp.exp(st[r, z, 0:1, :] - top) / total * n_v[r : r + 1, :].astype(F32)
        log_total = top + jnp.log(total)
        if r == 0:
            lt[l, :, :] = log_total
        else:
            lt[l, :, :] += log_total

    def weights(r, g):
        factor = sc_v[r]
        parts = []
        for i in range(g * 128, g * 128 + 128, 32):
            w = (e_v[r, i : i + 32, :] * factor).astype(jnp.bfloat16)
            w_v[r % 2, i : i + 32, :] = w
            w = w.astype(F32)
            part = w[:, :128]
            for k in range(128, N, 128):
                part = part + w[:, k : k + 128]
            parts.append(part)
        part = jnp.concatenate(parts, axis=0).T
        mass[p, r * 4 + g : r * 4 + g + 1, :] = jnp.sum(part, axis=0, keepdims=True)

    def moments(r, g):
        xx = (x + OFFS[g]) % 4
        lo = pl.ds(pl.multiple_of(xx * 128, 128), 128)
        hi = pl.ds(pl.multiple_of(512 + xx * 128, 128), 128)
        block = jnp.concatenate([p_v[:, lo], p_v[:, hi]], axis=1)
        out = jnp.dot(w_v[r % 2], block, preferred_element_type=F32)
        for h in range(2):
            part = out[:, h * 128 : (h + 1) * 128]
            zero, one = pack(part[:HALF], part[HALF:])
            mp[r, 0, xx, h, :, :] = zero
            mp[r, 1, xx, h, :, :] = one

    cc = {}

    def send_moments(r, g):
        xx = (x + OFFS[g]) % 4
        cc[r, g] = send(mp.at[r, 1 - c, xx], cr.at[r, xx], cs.at[r, g], crs.at[r, g], sib)

    xc = {}

    def xsend(r, i, src, dst, dev):
        xc[r, i] = send(src, dst, xs.at[r, i], xr.at[r, i], dev)

    x_opp, x_next, x_prev = (x + 2) % 4, (x + 1) % 4, (x + 3) % 4

    def own_centroids(r):
        q = pl.ds(pl.multiple_of((yh * 4 + x) * 128, 128), 128)
        zero, one = pack(c_v[r, :HALF, q].astype(F32), c_v[r, HALF:, q].astype(F32))
        return prior_weight * jnp.where(jnp.full((HALF, 128), c, jnp.int32) == 0, zero, one)

    def sum_cores(r, g):
        xx = (x + OFFS[g]) % 4
        for h in range(2):
            sa[r, xx, h, :, :] = mp[r, c, xx, h, :RA, :] + cr[r, xx, h, :RA, :]
            sb[r, h, xx, :, :] = mp[r, c, xx, h, RA:, :] + cr[r, xx, h, RA:, :]
        if g == 3:
            own = own_centroids(r)
            sa[r, x, yh, :, :] += own[:RA]
            sb[r, yh, x, :, :] += own[RA:]

    def send_cores(r, g):
        if g == 0:
            xsend(r, REL_P, sa.at[r, x_opp, 0], ra_m.at[r], xp)
            xsend(r, REL_M, sa.at[r, x_opp, 1], ra_p.at[r], xm)
        if g == 1:
            xsend(r, PLA_P, sa.at[r, x_next, 1], da_m.at[r, 1], xp)
        if g == 2:
            xsend(r, PLA_M, sa.at[r, x_prev, 0], da_p.at[r, 0], xm)
        xx = (x + OFFS[g]) % 4
        xsend(r, Y_B + g, sb.at[r, 1 - yh, xx], yb.at[r, xx], y2)

    def aug_a(r):
        xc[r, REL_P].wait_recv()
        sa[r, x_next, 0, :, :] += ra_m[r]
        xsend(r, AUG_P, sa.at[r, x_next, 0], da_m.at[r, 0], xp)
        xc[r, REL_M].wait_recv()
        sa[r, x_prev, 1, :, :] += ra_p[r]
        xsend(r, AUG_M, sa.at[r, x_prev, 1], da_p.at[r, 1], xm)

    def rel_b(r):
        xc[r, Y_B].wait_recv()
        sb[r, yh, x_opp, :, :] += yb[r, x_opp]
        xsend(r, BREL_P, sb.at[r, yh, x_opp, pl.ds(0, HB)], rb_m.at[r], xp)
        xsend(r, BREL_M, sb.at[r, yh, x_opp, pl.ds(HB, HB)], rb_p.at[r], xm)
        xc[r, Y_B + 1].wait_recv()
        sb[r, yh, x_next, :, :] += yb[r, x_next]
        xsend(r, BPLA_P, sb.at[r, yh, x_next, pl.ds(HB, HB)], db_m.at[r, pl.ds(HB, HB)], xp)
        xc[r, Y_B + 2].wait_recv()
        sb[r, yh, x_prev, :, :] += yb[r, x_prev]
        xsend(r, BPLA_M, sb.at[r, yh, x_prev, pl.ds(0, HB)], db_p.at[r, pl.ds(0, HB)], xm)
        xc[r, Y_B + 3].wait_recv()
        sb[r, yh, x, :, :] += yb[r, x]

    def y_a(r):
        for i in (PLA_P, PLA_M, AUG_P, AUG_M):
            xc[r, i].wait_recv()
        sa[r, x, 1 - yh, :, :] += da_m[r, 1 - yh] + da_p[r, 1 - yh]
        xsend(r, Y_A, sa.at[r, x, 1 - yh], ya.at[r], y2)
        sa[r, x, yh, :, :] += da_m[r, yh] + da_p[r, yh]

    def aug_b(r):
        xc[r, BREL_P].wait_recv()
        sb[r, yh, x_next, :HB, :] += rb_m[r]
        xsend(r, BAUG_P, sb.at[r, yh, x_next, pl.ds(0, HB)], db_m.at[r, pl.ds(0, HB)], xp)
        xc[r, BREL_M].wait_recv()
        sb[r, yh, x_prev, HB:, :] += rb_p[r]
        xsend(r, BAUG_M, sb.at[r, yh, x_prev, pl.ds(HB, HB)], db_p.at[r, pl.ds(HB, HB)], xm)

    mc = {}

    def send_mass():
        for j in range(1, 16):
            mc[j] = send(mass.at[p], mass.at[p], ms.at[j], mr.at[j], ((p + j) % 16, z, l))
        mc[0] = send(lt.at[l], lt.at[l], ls, lr, other)

    masses = []

    def receive_mass():
        for j in range(1, 16):
            mc[j].wait_recv()
        total = mass[0]
        for j in range(1, 16):
            total += mass[j]
        masses.append(total)
        mc[0].wait_recv()
        b_ref[...] = (lt[0] + lt[1]) / 8.0 - math.log(4096)

    def finish(r):
        total = masses[0]
        row = [total[r * 4 + i : r * 4 + i + 1, :] + prior_weight for i in range(4)]
        weight = (jnp.concatenate(row[:2], axis=1), jnp.concatenate(row[2:], axis=1))
        for i in (Y_A, BPLA_P, BPLA_M, BAUG_P, BAUG_M):
            xc[r, i].wait_recv()
        high = sa[r, x, yh] + ya[r]
        low = sb[r, yh, x] + db_m[r] + db_p[r]
        moved = jnp.concatenate([high, low], axis=0).T
        for i in range(2):
            u_ref[r, :, i * HALF : (i + 1) * HALF] = (moved[i * 64 : i * 64 + 64] / weight[i]).astype(
                jnp.bfloat16
            )

    logits(0)
    pl.semaphore_wait(barrier, 23)
    send_stats(0)
    for r in range(1, REPS):
        logits(r)
        send_stats(r)
    loads[1].wait()
    steps = [(r, g) for r in range(REPS) for g in range(4)]
    stages = {"aug_a": aug_a, "rel_b": rel_b, "y_a": y_a, "aug_b": aug_b, "finish": finish}
    for i in range(len(steps) + LAG):
        late = steps[i - LAG] if i >= LAG else None
        if i < len(steps):
            r, g = steps[i]
            if g == 0:
                scale(r)
                for k in range(4):
                    weights(r, k)
            moments(r, g)
            send_moments(r, g)
        if late:
            cc[late].wait_recv()
            sum_cores(*late)
        if late:
            send_cores(*late)
        if i == 12:
            send_mass()
        for name, r in EARLY.get(i, ()):
            stages[name](r)
    receive_mass()
    for name, r in LATE:
        stages[name](r)
    for copy in sent:
        copy.wait_send()


def shards(points, centroids, counts):
    dma = pltpu.SemaphoreType.DMA
    packed, bagged = pl.pallas_call(
        kernel,
        out_shape=(
            pltpu.VMEM((REPS, 64, NK), jnp.bfloat16),
            pltpu.VMEM((1, N), F32),
        ),
        in_specs=[pl.BlockSpec(memory_space=pl.ANY)] * 3,
        out_specs=[pl.BlockSpec(memory_space=pltpu.VMEM)] * 2,
        scratch_shapes=[
            pltpu.VMEM((N, D), jnp.bfloat16),
            pltpu.VMEM((REPS, NK, D), jnp.bfloat16),
            pltpu.VMEM((REPS, N), jnp.int32),
            pltpu.VMEM((REPS, NK, N), F32),
            pltpu.VMEM((2, NK, N), jnp.bfloat16),
            pltpu.VMEM((NK, 128), F32),
            pltpu.VMEM((REPS, 1, N), F32),
            pltpu.VMEM((REPS, 8, 2, N), F32),
            pltpu.VMEM((REPS, 2, 4, 2, HALF, 128), F32),
            pltpu.VMEM((REPS, 4, 2, HALF, 128), F32),
            pltpu.VMEM((REPS, 4, 2, RA, 128), F32),
            pltpu.VMEM((REPS, 2, 4, RB, 128), F32),
            pltpu.VMEM((REPS, RA, 128), F32),
            pltpu.VMEM((REPS, RA, 128), F32),
            pltpu.VMEM((REPS, 2, RA, 128), F32),
            pltpu.VMEM((REPS, 2, RA, 128), F32),
            pltpu.VMEM((REPS, RA, 128), F32),
            pltpu.VMEM((REPS, 4, RB, 128), F32),
            pltpu.VMEM((REPS, HB, 128), F32),
            pltpu.VMEM((REPS, HB, 128), F32),
            pltpu.VMEM((REPS, RB, 128), F32),
            pltpu.VMEM((REPS, RB, 128), F32),
            pltpu.VMEM((16, 4 * REPS, 128), F32),
            pltpu.VMEM((2, 1, N), F32),
            dma((2 + REPS,)),
            dma((REPS, 8)),
            dma((REPS, 8)),
            dma((REPS, 4)),
            dma((REPS, 4)),
            dma((REPS, EXCHANGES)),
            dma((REPS, EXCHANGES)),
            dma((16,)),
            dma((16,)),
            dma,
            dma,
        ],
        compiler_params=pltpu.CompilerParams(
            collective_id=0, has_side_effects=True, vmem_limit_bytes=56 * 1024 * 1024
        ),
    )(points, centroids, counts)
    return packed.transpose(0, 2, 1), bagged.reshape(N)


def solution(mesh):
    return jax.shard_map(
        shards,
        mesh=mesh,
        in_specs=(P("dp", None), P("rep", "cent", None), P("rep", "dp")),
        out_specs=(P("rep", "cent", "dp"), P("dp")),
        check_vma=False,
    )
```

time: 62.6 us -> 54.5 us (0.87)
  Pallas kernels: 58.6 us -> 52.5 us
  local copies, waits for them, and re-layouts: 3.09 us -> 1.3 us
    pallas_call x1, Pallas kernels: 58.6 us -> 52.5 us  [shards(): pl.pallas_call(kernel, out_shape=(pltpu.VMEM((REPS, 64, NK), jnp.bfloat16...]
    pallas_call x1 -> x0, local copies, waits for them, and re-layouts: 1.09 us -> none  [shards(): pl.pallas_call(kernel, out_shape=(jax.ShapeDtypeStruct((REPS, HALF, 128),...]
    reshape x1 -> x0, local copies, waits for them, and re-layouts: 0.72 us -> none  [shards(): packed.reshape(REPS, HALF, 2, 64).transpose(0, 2, 1, 3)]
    unnamed x1 -> x2, local copies, waits for them, and re-layouts: 1.28 us -> 1.3 us
where the time goes in v2:
time: 54.5 us; the launch traced here: 54.4 us
  Pallas kernels  52.5 us (96%)
  local copies, waits for them, and re-layouts  1.3 us (2%)
  between operations  0.64 us (1%)
    pallas_call x1, Pallas kernels, shards(): pl.pallas_call(kernel, out_shape=(pltpu.VMEM((REPS, 64, NK), jnp.bfloat16...  52.5 us
    unnamed x2, local copies, waits for them, and re-layouts  1.3 us

profile of v2, /device:TPU:2, one launch (start us, length us, event | category | flops | bytes accessed | tf_op | source)
XLA Modules:
  0.0 54.4 jit_solution(1814729428577100838)
XLA Ops:
  0.6 52.5 %shard_map.50 = (bf16[4,64,512]{2,1,0:T(8,128)(2,1)S(1)}, f32[1,1024]{1,0:T(1,128)S(1)}) custom-call(bf16[1024,1024]{1,0:T(8,128)(2,1)} %p_hbm.1, bf16[4,512,1024]{2,1,0:T(8,128)(2,1)} %c_hbm.1, s32[4,1024]{1,0:T(4,128)} %n_hbm.1), custom_call_target="tpu_custom_call" | custom-call | tf_op jit(solution)/shard_map/pallas_call | solution.py:302
  53.1 0.7 %copy.7 = bf16[4,512,64]{1,2,0:T(8,128)(2,1)} copy(bf16[4,512,64]{1,2,0:T(8,128)(2,1)S(1)} %bitcast.2) | data formatting | bytes 524288
  53.8 0.6 %copy.8 = f32[1024]{0:T(1024)} copy(f32[1024]{0:T(1024)S(1)} %bitcast.3) | data formatting | bytes 8192

commit v3 on v2

--- a/solution.py
+++ b/solution.py
@@ -25,11 +25,11 @@
 REL_P, REL_M, PLA_P, PLA_M, AUG_P, AUG_M, Y_A, BREL_P, BREL_M, BPLA_P, BPLA_M, BAUG_P, BAUG_M, Y_B = range(14)
 EXCHANGES = Y_B + 4
 
-EARLY = {11: [("aug_a", 0)], 15: [("aug_a", 1)]}
+EARLY = {9: [("aug_a", 0)], 13: [("aug_a", 1)]}
 LATE = [
-    ("rel_b", 0), ("aug_a", 2), ("y_a", 0), ("rel_b", 1), ("aug_a", 3), ("aug_b", 0), ("y_a", 1), ("rel_b", 2),
-    ("aug_b", 1), ("y_a", 2), ("rel_b", 3), ("aug_b", 2), ("y_a", 3), ("finish", 0), ("finish", 1), ("aug_b", 3),
-    ("finish", 2), ("finish", 3),
+    ("rel_b", 0), ("aug_a", 2), ("mass_y", 0), ("y_a", 0), ("rel_b", 1), ("aug_a", 3), ("aug_b", 0), ("y_a", 1), ("rel_b", 2),
+    ("aug_b", 1), ("y_a", 2), ("rel_b", 3), ("aug_b", 2), ("y_a", 3), ("mass", 0), ("finish", 0), ("finish", 1),
+    ("aug_b", 3), ("finish", 2), ("finish", 3),
 ]
 
 
@@ -54,6 +54,7 @@
     sib = (p + 1 - 2 * c, z, l)
     xp = (yh * 8 + ((x + 1) % 4) * 2 + c, z, l)
     xm = (yh * 8 + ((x + 3) % 4) * 2 + c, z, l)
+    x2 = (yh * 8 + ((x + 2) % 4) * 2 + c, z, l)
     y2 = ((1 - yh) * 8 + x * 2 + c, z, l)
     other = (p, z, 1 - l)
 
@@ -65,11 +66,9 @@
         loads[i].start()
 
     barrier = pltpu.get_barrier_semaphore()
-    for j in range(1, 16):
-        pl.semaphore_signal(barrier, inc=1, device_id=((p + j) % 16, z, l), device_id_type=MESH)
-    for j in range(1, 8):
-        pl.semaphore_signal(barrier, inc=1, device_id=(p, (z + j) % 8, l), device_id_type=MESH)
-    pl.semaphore_signal(barrier, inc=1, device_id=other, device_id_type=MESH)
+    peers = [(p, (z + j) % 8, l) for j in (4, 3, 5, 2, 6, 1, 7)] + [x2, y2, xp, xm, sib, other]
+    for peer in peers:
+        pl.semaphore_signal(barrier, inc=1, device_id=peer, device_id_type=MESH)
 
     sent = []
 
@@ -139,7 +138,7 @@
                 part = part + w[:, k : k + 128]
             parts.append(part)
         part = jnp.concatenate(parts, axis=0).T
-        mass[p, r * 4 + g : r * 4 + g + 1, :] = jnp.sum(part, axis=0, keepdims=True)
+        mass[0, r * 4 + g : r * 4 + g + 1, :] = jnp.sum(part, axis=0, keepdims=True)
 
     def moments(r, g):
         xx = (x + OFFS[g]) % 4
@@ -231,21 +230,31 @@
 
     mc = {}
 
-    def send_mass():
-        for j in range(1, 16):
-            mc[j] = send(mass.at[p], mass.at[p], ms.at[j], mr.at[j], ((p + j) % 16, z, l))
-        mc[0] = send(lt.at[l], lt.at[l], ls, lr, other)
+    def mass_send(i, src, dst, dev):
+        mc[i] = send(mass.at[src], mass.at[dst], ms.at[i], mr.at[i], dev)
+
+    def mass_core():
+        mass_send(0, 0, 1, sib)
+        mc["lt"] = send(lt.at[l], lt.at[l], ls, lr, other)
+
+    def mass_x():
+        mc[0].wait_recv()
+        mass[2, :, :] = mass[0] + mass[1]
+        for j, dev in ((1, xp), (2, x2), (3, xm)):
+            mass_send(j, 2, 2 + j, dev)
+
+    def mass_y():
+        for j in (1, 2, 3):
+            mc[j].wait_recv()
+        mass[6, :, :] = mass[2] + mass[3] + mass[4] + mass[5]
+        mass_send(4, 6, 7, y2)
 
     masses = []
 
     def receive_mass():
-        for j in range(1, 16):
-            mc[j].wait_recv()
-        total = mass[0]
-        for j in range(1, 16):
-            total += mass[j]
-        masses.append(total)
-        mc[0].wait_recv()
+        mc[4].wait_recv()
+        masses.append(mass[6] + mass[7])
+        mc["lt"].wait_recv()
         b_ref[...] = (lt[0] + lt[1]) / 8.0 - math.log(4096)
 
     def finish(r):
@@ -263,7 +272,7 @@
             )
 
     logits(0)
-    pl.semaphore_wait(barrier, 23)
+    pl.semaphore_wait(barrier, len(peers))
     send_stats(0)
     for r in range(1, REPS):
         logits(r)
@@ -287,12 +296,18 @@
         if late:
             send_cores(*late)
         if i == 12:
-            send_mass()
+            mass_core()
+        if i == 15:
+            mass_x()
         for name, r in EARLY.get(i, ()):
             stages[name](r)
-    receive_mass()
     for name, r in LATE:
-        stages[name](r)
+        if name == "mass_y":
+            mass_y()
+        elif name == "mass":
+            receive_mass()
+        else:
+            stages[name](r)
     for copy in sent:
         copy.wait_send()
 
@@ -330,7 +345,7 @@
             pltpu.VMEM((REPS, HB, 128), F32),
             pltpu.VMEM((REPS, RB, 128), F32),
             pltpu.VMEM((REPS, RB, 128), F32),
-            pltpu.VMEM((16, 4 * REPS, 128), F32),
+            pltpu.VMEM((8, 4 * REPS, 128), F32),
             pltpu.VMEM((2, 1, N), F32),
             dma((2 + REPS,)),
             dma((REPS, 8)),
@@ -339,8 +354,8 @@
             dma((REPS, 4)),
             dma((REPS, EXCHANGES)),
             dma((REPS, EXCHANGES)),
-            dma((16,)),
-            dma((16,)),
+            dma((5,)),
+            dma((5,)),
             dma,
             dma,
         ],

time: 54.5 us -> 52.6 us (0.965)
  Pallas kernels: 52.5 us -> 50.5 us
    pallas_call x1, Pallas kernels: 52.5 us -> 50.5 us  [shards(): pl.pallas_call(kernel, out_shape=(pltpu.VMEM((REPS, 64, NK), jnp.bfloat16...]
where the time goes in v3:
time: 52.6 us; the launch traced here: 52.5 us
  Pallas kernels  50.5 us (96%)
  local copies, waits for them, and re-layouts  1.3 us (2%)
  between operations  0.64 us (1%)
    pallas_call x1, Pallas kernels, shards(): pl.pallas_call(kernel, out_shape=(pltpu.VMEM((REPS, 64, NK), jnp.bfloat16...  50.5 us
    unnamed x2, local copies, waits for them, and re-layouts  1.3 us

profile of v3, /device:TPU:2, one launch (start us, length us, event | category | flops | bytes accessed | tf_op | source)
XLA Modules:
  0.0 52.5 jit_solution(11507046016747341270)
XLA Ops:
  0.6 50.5 %shard_map.50 = (bf16[4,64,512]{2,1,0:T(8,128)(2,1)S(1)}, f32[1,1024]{1,0:T(1,128)S(1)}) custom-call(bf16[1024,1024]{1,0:T(8,128)(2,1)} %p_hbm.1, bf16[4,512,1024]{2,1,0:T(8,128)(2,1)} %c_hbm.1, s32[4,1024]{1,0:T(4,128)} %n_hbm.1), custom_call_target="tpu_custom_call" | custom-call | tf_op jit(solution)/shard_map/pallas_call | solution.py:317
  51.2 0.7 %copy.7 = bf16[4,512,64]{1,2,0:T(8,128)(2,1)} copy(bf16[4,512,64]{1,2,0:T(8,128)(2,1)S(1)} %bitcast.2) | data formatting | bytes 524288
  51.9 0.6 %copy.8 = f32[1024]{0:T(1024)} copy(f32[1024]{0:T(1024)S(1)} %bitcast.3) | data formatting | bytes 8192

commit v4 on v3

--- a/solution.py
+++ b/solution.py
@@ -18,7 +18,7 @@
 RB = HALF - RA
 HB = RB // 2
 NT = 256
-LAG = 3
+LAG = 2
 OFFS = (2, 1, 3, 0)
 prior_weight = 1.0
 
@@ -27,9 +27,9 @@
 
 EARLY = {9: [("aug_a", 0)], 13: [("aug_a", 1)]}
 LATE = [
-    ("rel_b", 0), ("aug_a", 2), ("mass_y", 0), ("y_a", 0), ("rel_b", 1), ("aug_a", 3), ("aug_b", 0), ("y_a", 1), ("rel_b", 2),
-    ("aug_b", 1), ("y_a", 2), ("rel_b", 3), ("aug_b", 2), ("y_a", 3), ("mass", 0), ("finish", 0), ("finish", 1),
-    ("aug_b", 3), ("finish", 2), ("finish", 3),
+    ("aug_a", 2), ("rel_b", 0), ("mass_y", 0), ("y_a", 0), ("aug_a", 3), ("rel_b", 1), ("y_a", 1), ("aug_b", 0),
+    ("rel_b", 2), ("y_a", 2), ("aug_b", 1), ("rel_b", 3), ("y_a", 3), ("aug_b", 2), ("aug_b", 3), ("mass", 0),
+    ("finish", 0), ("finish", 1), ("finish", 2), ("finish", 3),
 ]
 
 

time: 52.6 us -> 51.7 us (0.983)
  Pallas kernels: 50.5 us -> 49.7 us
    pallas_call x1, Pallas kernels: 50.5 us -> 49.7 us  [shards(): pl.pallas_call(kernel, out_shape=(pltpu.VMEM((REPS, 64, NK), jnp.bfloat16...]
where the time goes in v4:
time: 51.7 us; the launch traced here: 51.6 us
  Pallas kernels  49.7 us (96%)
  local copies, waits for them, and re-layouts  1.3 us (3%)
  between operations  0.64 us (1%)
    pallas_call x1, Pallas kernels, shards(): pl.pallas_call(kernel, out_shape=(pltpu.VMEM((REPS, 64, NK), jnp.bfloat16...  49.7 us
    unnamed x2, local copies, waits for them, and re-layouts  1.3 us

profile of v4, /device:TPU:2, one launch (start us, length us, event | category | flops | bytes accessed | tf_op | source)
XLA Modules:
  0.0 51.6 jit_solution(16519748799303226272)
XLA Ops:
  0.6 49.7 %shard_map.50 = (bf16[4,64,512]{2,1,0:T(8,128)(2,1)S(1)}, f32[1,1024]{1,0:T(1,128)S(1)}) custom-call(bf16[1024,1024]{1,0:T(8,128)(2,1)} %p_hbm.1, bf16[4,512,1024]{2,1,0:T(8,128)(2,1)} %c_hbm.1, s32[4,1024]{1,0:T(4,128)} %n_hbm.1), custom_call_target="tpu_custom_call" | custom-call | tf_op jit(solution)/shard_map/pallas_call | solution.py:317
  50.3 0.7 %copy.7 = bf16[4,512,64]{1,2,0:T(8,128)(2,1)} copy(bf16[4,512,64]{1,2,0:T(8,128)(2,1)S(1)} %bitcast.2) | data formatting | bytes 524288
  51.0 0.6 %copy.8 = f32[1024]{0:T(1024)} copy(f32[1024]{0:T(1024)S(1)} %bitcast.3) | data formatting | bytes 8192

commit v5 on v4

--- a/solution.py
+++ b/solution.py
@@ -14,8 +14,9 @@
 HALF = 256
 D = 1024
 N = 1024
-RA = 144
-RB = HALF - RA
+SPLIT = (160, 144, 144, 128)
+RA = max(SPLIT)
+RB = HALF - min(SPLIT)
 HB = RB // 2
 NT = 256
 LAG = 2
@@ -141,16 +142,19 @@
         mass[0, r * 4 + g : r * 4 + g + 1, :] = jnp.sum(part, axis=0, keepdims=True)
 
     def moments(r, g):
-        xx = (x + OFFS[g]) % 4
-        lo = pl.ds(pl.multiple_of(xx * 128, 128), 128)
-        hi = pl.ds(pl.multiple_of(512 + xx * 128, 128), 128)
-        block = jnp.concatenate([p_v[:, lo], p_v[:, hi]], axis=1)
-        out = jnp.dot(w_v[r % 2], block, preferred_element_type=F32)
-        for h in range(2):
-            part = out[:, h * 128 : (h + 1) * 128]
+        if g % 2:
+            return
+        spots = [(x + OFFS[g]) % 4, (x + OFFS[g + 1]) % 4]
+        blocks = []
+        for xx in spots:
+            blocks.append(p_v[:, pl.ds(pl.multiple_of(xx * 128, 128), 128)])
+            blocks.append(p_v[:, pl.ds(pl.multiple_of(512 + xx * 128, 128), 128)])
+        out = jnp.dot(w_v[r % 2], jnp.concatenate(blocks, axis=1), preferred_element_type=F32)
+        for k in range(4):
+            part = out[:, k * 128 : (k + 1) * 128]
             zero, one = pack(part[:HALF], part[HALF:])
-            mp[r, 0, xx, h, :, :] = zero
-            mp[r, 1, xx, h, :, :] = one
+            mp[r, 0, spots[k // 2], k % 2, :, :] = zero
+            mp[r, 1, spots[k // 2], k % 2, :, :] = one
 
     cc = {}
 
@@ -171,62 +175,74 @@
         return prior_weight * jnp.where(jnp.full((HALF, 128), c, jnp.int32) == 0, zero, one)
 
     def sum_cores(r, g):
+        ra, hb = SPLIT[r], (HALF - SPLIT[r]) // 2
+        rb = 2 * hb
         xx = (x + OFFS[g]) % 4
         for h in range(2):
-            sa[r, xx, h, :, :] = mp[r, c, xx, h, :RA, :] + cr[r, xx, h, :RA, :]
-            sb[r, h, xx, :, :] = mp[r, c, xx, h, RA:, :] + cr[r, xx, h, RA:, :]
+            sa[r, xx, h, :ra, :] = mp[r, c, xx, h, :ra, :] + cr[r, xx, h, :ra, :]
+            sb[r, h, xx, :rb, :] = mp[r, c, xx, h, ra:, :] + cr[r, xx, h, ra:, :]
         if g == 3:
             own = own_centroids(r)
-            sa[r, x, yh, :, :] += own[:RA]
-            sb[r, yh, x, :, :] += own[RA:]
+            sa[r, x, yh, :ra, :] += own[:ra]
+            sb[r, yh, x, :rb, :] += own[ra:]
 
     def send_cores(r, g):
+        ra, hb = SPLIT[r], (HALF - SPLIT[r]) // 2
+        rb = 2 * hb
         if g == 0:
-            xsend(r, REL_P, sa.at[r, x_opp, 0], ra_m.at[r], xp)
-            xsend(r, REL_M, sa.at[r, x_opp, 1], ra_p.at[r], xm)
+            xsend(r, REL_P, sa.at[r, x_opp, 0, pl.ds(0, ra)], ra_m.at[r, pl.ds(0, ra)], xp)
+            xsend(r, REL_M, sa.at[r, x_opp, 1, pl.ds(0, ra)], ra_p.at[r, pl.ds(0, ra)], xm)
         if g == 1:
-            xsend(r, PLA_P, sa.at[r, x_next, 1], da_m.at[r, 1], xp)
+            xsend(r, PLA_P, sa.at[r, x_next, 1, pl.ds(0, ra)], da_m.at[r, 1, pl.ds(0, ra)], xp)
         if g == 2:
-            xsend(r, PLA_M, sa.at[r, x_prev, 0], da_p.at[r, 0], xm)
+            xsend(r, PLA_M, sa.at[r, x_prev, 0, pl.ds(0, ra)], da_p.at[r, 0, pl.ds(0, ra)], xm)
         xx = (x + OFFS[g]) % 4
-        xsend(r, Y_B + g, sb.at[r, 1 - yh, xx], yb.at[r, xx], y2)
+        xsend(r, Y_B + g, sb.at[r, 1 - yh, xx, pl.ds(0, rb)], yb.at[r, xx, pl.ds(0, rb)], y2)
 
     def aug_a(r):
+        ra, hb = SPLIT[r], (HALF - SPLIT[r]) // 2
+        rb = 2 * hb
         xc[r, REL_P].wait_recv()
-        sa[r, x_next, 0, :, :] += ra_m[r]
-        xsend(r, AUG_P, sa.at[r, x_next, 0], da_m.at[r, 0], xp)
+        sa[r, x_next, 0, :ra, :] += ra_m[r, :ra]
+        xsend(r, AUG_P, sa.at[r, x_next, 0, pl.ds(0, ra)], da_m.at[r, 0, pl.ds(0, ra)], xp)
         xc[r, REL_M].wait_recv()
-        sa[r, x_prev, 1, :, :] += ra_p[r]
-        xsend(r, AUG_M, sa.at[r, x_prev, 1], da_p.at[r, 1], xm)
+        sa[r, x_prev, 1, :ra, :] += ra_p[r, :ra]
+        xsend(r, AUG_M, sa.at[r, x_prev, 1, pl.ds(0, ra)], da_p.at[r, 1, pl.ds(0, ra)], xm)
 
     def rel_b(r):
+        ra, hb = SPLIT[r], (HALF - SPLIT[r]) // 2
+        rb = 2 * hb
         xc[r, Y_B].wait_recv()
-        sb[r, yh, x_opp, :, :] += yb[r, x_opp]
-        xsend(r, BREL_P, sb.at[r, yh, x_opp, pl.ds(0, HB)], rb_m.at[r], xp)
-        xsend(r, BREL_M, sb.at[r, yh, x_opp, pl.ds(HB, HB)], rb_p.at[r], xm)
+        sb[r, yh, x_opp, :rb, :] += yb[r, x_opp, :rb]
+        xsend(r, BREL_P, sb.at[r, yh, x_opp, pl.ds(0, hb)], rb_m.at[r, pl.ds(0, hb)], xp)
+        xsend(r, BREL_M, sb.at[r, yh, x_opp, pl.ds(hb, hb)], rb_p.at[r, pl.ds(0, hb)], xm)
         xc[r, Y_B + 1].wait_recv()
-        sb[r, yh, x_next, :, :] += yb[r, x_next]
-        xsend(r, BPLA_P, sb.at[r, yh, x_next, pl.ds(HB, HB)], db_m.at[r, pl.ds(HB, HB)], xp)
+        sb[r, yh, x_next, :rb, :] += yb[r, x_next, :rb]
+        xsend(r, BPLA_P, sb.at[r, yh, x_next, pl.ds(hb, hb)], db_m.at[r, pl.ds(hb, hb)], xp)
         xc[r, Y_B + 2].wait_recv()
-        sb[r, yh, x_prev, :, :] += yb[r, x_prev]
-        xsend(r, BPLA_M, sb.at[r, yh, x_prev, pl.ds(0, HB)], db_p.at[r, pl.ds(0, HB)], xm)
+        sb[r, yh, x_prev, :rb, :] += yb[r, x_prev, :rb]
+        xsend(r, BPLA_M, sb.at[r, yh, x_prev, pl.ds(0, hb)], db_p.at[r, pl.ds(0, hb)], xm)
         xc[r, Y_B + 3].wait_recv()
-        sb[r, yh, x, :, :] += yb[r, x]
+        sb[r, yh, x, :rb, :] += yb[r, x, :rb]
 
     def y_a(r):
+        ra, hb = SPLIT[r], (HALF - SPLIT[r]) // 2
+        rb = 2 * hb
         for i in (PLA_P, PLA_M, AUG_P, AUG_M):
             xc[r, i].wait_recv()
-        sa[r, x, 1 - yh, :, :] += da_m[r, 1 - yh] + da_p[r, 1 - yh]
-        xsend(r, Y_A, sa.at[r, x, 1 - yh], ya.at[r], y2)
-        sa[r, x, yh, :, :] += da_m[r, yh] + da_p[r, yh]
+        sa[r, x, 1 - yh, :ra, :] += da_m[r, 1 - yh, :ra] + da_p[r, 1 - yh, :ra]
+        xsend(r, Y_A, sa.at[r, x, 1 - yh, pl.ds(0, ra)], ya.at[r, pl.ds(0, ra)], y2)
+        sa[r, x, yh, :ra, :] += da_m[r, yh, :ra] + da_p[r, yh, :ra]
 
     def aug_b(r):
+        ra, hb = SPLIT[r], (HALF - SPLIT[r]) // 2
+        rb = 2 * hb
         xc[r, BREL_P].wait_recv()
-        sb[r, yh, x_next, :HB, :] += rb_m[r]
-        xsend(r, BAUG_P, sb.at[r, yh, x_next, pl.ds(0, HB)], db_m.at[r, pl.ds(0, HB)], xp)
+        sb[r, yh, x_next, :hb, :] += rb_m[r, :hb]
+        xsend(r, BAUG_P, sb.at[r, yh, x_next, pl.ds(0, hb)], db_m.at[r, pl.ds(0, hb)], xp)
         xc[r, BREL_M].wait_recv()
-        sb[r, yh, x_prev, HB:, :] += rb_p[r]
-        xsend(r, BAUG_M, sb.at[r, yh, x_prev, pl.ds(HB, HB)], db_p.at[r, pl.ds(HB, HB)], xm)
+        sb[r, yh, x_prev, hb:rb, :] += rb_p[r, :hb]
+        xsend(r, BAUG_M, sb.at[r, yh, x_prev, pl.ds(hb, hb)], db_p.at[r, pl.ds(hb, hb)], xm)
 
     mc = {}
 
@@ -258,13 +274,15 @@
         b_ref[...] = (lt[0] + lt[1]) / 8.0 - math.log(4096)
 
     def finish(r):
+        ra, hb = SPLIT[r], (HALF - SPLIT[r]) // 2
+        rb = 2 * hb
         total = masses[0]
         row = [total[r * 4 + i : r * 4 + i + 1, :] + prior_weight for i in range(4)]
         weight = (jnp.concatenate(row[:2], axis=1), jnp.concatenate(row[2:], axis=1))
         for i in (Y_A, BPLA_P, BPLA_M, BAUG_P, BAUG_M):
             xc[r, i].wait_recv()
-        high = sa[r, x, yh] + ya[r]
-        low = sb[r, yh, x] + db_m[r] + db_p[r]
+        high = sa[r, x, yh, :ra] + ya[r, :ra]
+        low = sb[r, yh, x, :rb] + db_m[r, :rb] + db_p[r, :rb]
         moved = jnp.concatenate([high, low], axis=0).T
         for i in range(2):
             u_ref[r, :, i * HALF : (i + 1) * HALF] = (moved[i * 64 : i * 64 + 64] / weight[i]).astype(

time: 51.7 us -> 51.6 us (level)
  no operation moved by 1% of the time
where the time goes in v5:
time: 51.6 us; the launch traced here: 51.5 us
  Pallas kernels  49.5 us (96%)
  local copies, waits for them, and re-layouts  1.3 us (3%)
  between operations  0.64 us (1%)
    pallas_call x1, Pallas kernels, shards(): pl.pallas_call(kernel, out_shape=(pltpu.VMEM((REPS, 64, NK), jnp.bfloat16...  49.5 us
    unnamed x2, local copies, waits for them, and re-layouts  1.3 us

profile of v5, /device:TPU:2, one launch (start us, length us, event | category | flops | bytes accessed | tf_op | source)
XLA Modules:
  0.0 51.5 jit_solution(15754593837890452488)
XLA Ops:
  0.6 49.5 %shard_map.50 = (bf16[4,64,512]{2,1,0:T(8,128)(2,1)S(1)}, f32[1,1024]{1,0:T(1,128)S(1)}) custom-call(bf16[1024,1024]{1,0:T(8,128)(2,1)} %p_hbm.1, bf16[4,512,1024]{2,1,0:T(8,128)(2,1)} %c_hbm.1, s32[4,1024]{1,0:T(4,128)} %n_hbm.1), custom_call_target="tpu_custom_call" | custom-call | tf_op jit(solution)/shard_map/pallas_call | solution.py:335
  50.2 0.7 %copy.7 = bf16[4,512,64]{1,2,0:T(8,128)(2,1)} copy(bf16[4,512,64]{1,2,0:T(8,128)(2,1)S(1)} %bitcast.2) | data formatting | bytes 524288
  50.9 0.6 %copy.8 = f32[1024]{0:T(1024)} copy(f32[1024]{0:T(1024)S(1)} %bitcast.3) | data formatting | bytes 8192
